TPU v7x, 32 devices: a whole 2x2x4 slice. The times are simulated.
32 devices in a mesh: cell: 2 (over y), row: 16 (over z, x, core).
Axes of the slice: x: 2, y: 2, z: 4, core: 2. Of those that a mesh axis runs over, the one named last changes fastest.
Arguments:
- e_blocks: bfloat16 [128, 4, 128, 128], P(('cell', 'row')), parts along dimension 0, may hold values from -0.0625 to 0.0625
- e_cols: int32 [128, 4], P('cell'), parts along dimension 0, may hold values from 0 to 63, as said below
- p1_blocks: bfloat16 [128, 4, 128, 128], P(('cell', 'row')), parts along dimension 0, may hold values from -6 to 6
- p1_cols: int32 [128, 4], P('cell'), parts along dimension 0, may hold values from 0 to 63, as said below
- dh_owned: bfloat16 [384, 128, 128], P(('cell', 'row')), parts along dimension 0, may hold values from -6 to 6
- dh_source: int32 [128, 3], P(('cell', 'row')), parts along dimension 0, may hold values from 0 to 191, as said below
- dh_slot: int32 [128, 3], P(('cell', 'row')), parts along dimension 0, may hold values from 0 to 3, as said below
Outputs:
- e_out: float32 [128, 4, 128, 128], P(('cell', 'row')), parts along dimension 0
- p1_out: float32 [128, 4, 128, 128], P(('cell', 'row')), parts along dimension 0
There are 2 independent parts, one for each index of `cell`. A program takes and returns all parts, laid end to end along the dimension named above; each array names one. Nothing has to cross between parts.
Inputs may be any that keep to these rules, and one draw needn't show every extreme that they name: `e_cols`: in every block row i the 4 columns are distinct and lie within 4 block rows of i, cyclically modulo 64; both offsets -4 and +4 occur. `p1_cols`: in every block row i the 4 columns are distinct and lie within 4 block rows of i, cyclically modulo 64; both offsets -4 and +4 occur. `dh_source`: A permutation of the owner-order positions. Owner-order position q lies on device q // 12; the block of block row i comes from the device of row i or from one of its two neighbours along the axis (cyclically), each device owning as many blocks of its own rows as of each neighbour's. `dh_slot`: the 3 slots of a block row are distinct.
All inputs are finite; a program needn't handle non-finite values.
Results may differ from a plain program's by a relative error of at most 0.00088.
Values may be sent and summed in bfloat16 or wider, within the bound.
A program may use at most 64 MiB of HBM per device.

v0:
```python
import math

import jax
import jax.numpy as jnp
from jax import lax
from jax.sharding import PartitionSpec as P

BLK = 128
REACH = 4
KB = 4
ITERS = 2


def with_halo(shard, sides, width):
    for axis, dim in sides:
        size, length = (lax.axis_size(axis), shard.shape[dim])
        up = [(i, (i + 1) % size) for i in range(size)]
        down = [(j, i) for i, j in up]
        last = lax.slice_in_dim(shard, length - width, length, axis=dim)
        leading = lax.slice_in_dim(shard, 0, width, axis=dim)
        before = lax.ppermute(last, axis, up)
        after = lax.ppermute(leading, axis, down)
        shard = jnp.concatenate([before, shard, after], axis=dim)
    return shard


def shifted(value, axis, steps):
    count = lax.axis_size(axis)
    pairs = [(source, (source + steps) % count) for source in range(count)]
    return lax.ppermute(value, axis, pairs)


def widen_cols(cols, row_start, rows_here):
    total_rows = cols.shape[0]
    wanted = (row_start - REACH + jnp.arange(rows_here + 2 * REACH, dtype=jnp.int32)) % total_rows
    return jnp.take(cols, wanted, axis=0)


def multiply(left_blocks, left_cols, right_wide, right_cols, target_cols, row_start, total_rows):
    right_count = right_cols.shape[1]
    block_size = right_wide.shape[-1]
    local_rows = (left_cols - row_start + REACH) % total_rows
    held_cols = jnp.take(right_cols, local_rows, axis=0)
    matches = held_cols[:, :, :, None] == target_cols[:, None, None, :]
    present = jnp.any(matches, axis=2)
    positions = jnp.arange(right_count, dtype=jnp.int32)[None, None, :, None]
    slot_pos = jnp.sum(jnp.where(matches, positions, 0), axis=2)
    flat_pos = local_rows[:, :, None] * right_count + slot_pos
    picked = jnp.take(right_wide.reshape(-1, block_size, block_size), flat_pos, axis=0)
    picked = jnp.where(present[:, :, :, None, None], picked, jnp.zeros((), picked.dtype))
    return jnp.einsum("rkab,rknbc->rnac", left_blocks, picked, preferred_element_type=jnp.float32)


def fetch_once(blocks):
    return with_halo(blocks, (("row", 0),), REACH)


def body(e_blocks, e_cols, p1_blocks, p1_cols, dh_owned, dh_source, dh_slot):
    rows_here = e_blocks.shape[0]
    total_rows = e_cols.shape[0]
    device_pos = lax.axis_index("row")
    devices = lax.axis_size("row")
    row_start = device_pos * rows_here
    dev_cols = lax.dynamic_slice_in_dim(e_cols, row_start, rows_here, 0)
    resp_cols = lax.dynamic_slice_in_dim(p1_cols, row_start, rows_here, 0)
    dev_wide_cols = widen_cols(e_cols, row_start, rows_here)
    resp_wide_cols = widen_cols(p1_cols, row_start, rows_here)
    owned_count = dh_owned.shape[0]
    from_lower = shifted(dh_owned, "row", 1)
    from_upper = shifted(dh_owned, "row", -1)
    nearby = jnp.concatenate([from_lower, dh_owned, from_upper], axis=0)
    owner_dev = dh_source // owned_count
    relative = (owner_dev - device_pos + 1) % devices
    nearby_pos = relative * owned_count + dh_source % owned_count
    dh_rows = jnp.take(nearby, nearby_pos, axis=0)
    slot_table = (dh_slot[:, :, None] == jnp.arange(KB, dtype=jnp.int32)[None, None, :]).astype(
        jnp.bfloat16
    )
    response = p1_blocks.astype(jnp.float32) + jnp.einsum(
        "rum,ruab->rmab", slot_table, dh_rows, preferred_element_type=jnp.float32
    )
    deviation = e_blocks.astype(jnp.float32)

    def product(left_blocks, left_cols, right_wide, right_cols, target_cols):
        return multiply(
            left_blocks, left_cols, right_wide, right_cols, target_cols, row_start, total_rows
        )

    for iteration in range(ITERS):
        deviation_half = deviation.astype(jnp.bfloat16)
        response_half = response.astype(jnp.bfloat16)
        deviation_wide = fetch_once(deviation_half)
        response_wide = fetch_once(response_half)
        square = product(deviation_half, dev_cols, deviation_wide, dev_wide_cols, dev_cols).astype(
            jnp.bfloat16
        )
        cube_term = product(square, dev_cols, deviation_wide, dev_wide_cols, dev_cols)
        left_product = product(
            deviation_half, dev_cols, response_wide, resp_wide_cols, resp_cols
        ).astype(jnp.bfloat16)
        middle = product(left_product, resp_cols, deviation_wide, dev_wide_cols, resp_cols)
        front_term = product(square, dev_cols, response_wide, resp_wide_cols, resp_cols)
        back_term = product(response_half, resp_cols, fetch_once(square), dev_wide_cols, resp_cols)
        response = 1.5 * response - 2.0 * (front_term + middle + back_term)
        deviation = 1.5 * deviation - 2.0 * cube_term
    return (deviation * math.sqrt(KB * BLK), response)


def solution(mesh):
    in_specs = (
        P(("cell", "row"), None, None, None),
        P("cell", None),
        P(("cell", "row"), None, None, None),
        P("cell", None),
        P(("cell", "row"), None, None),
        P(("cell", "row"), None),
        P(("cell", "row"), None),
    )
    out_specs = (P(("cell", "row"), None, None, None), P(("cell", "row"), None, None, None))
    return jax.shard_map(body, mesh=mesh, in_specs=in_specs, out_specs=out_specs, check_vma=False)
```

profile of v0, /device:TPU:0, one launch (start us, length us, event | category | flops | bytes accessed | tf_op | source)
XLA Modules:
  0.0 119.4 jit_solution(6672142153458163353)
XLA Ops:
  0.6 0.5 collective-permute-start.4
  1.2 5.0 %collective-permute-start.5 = (bf16[12,128,128]{2,1,0:T(8,128)(2,1)}, bf16[12,128,128]{2,1,0:T(8,128)(2,1)S(1)}, u32[]{:S(2)}, u32[]{:S(2)}) collective-permute-start(bf16[12,128,128]{2,1,0:T(8,128)(2,1)} %param.17), channel_id=1, source_target_pairs={{0,15},{1,0},{2,1},{3,2},{4,3},{5,4},{6,5},{7,6},{8,7},{9,8},{10,9... | collective-permute-start | bytes 1179656 | tf_op jit(solution)/shard_map/ppermute | solution.py:30
  6.2 4.4 %collective-permute-start.1 = (bf16[4,4,128,128]{3,2,1,0:T(8,128)(2,1)}, bf16[4,4,128,128]{3,2,1,0:T(8,128)(2,1)}, u32[]{:S(2)}, u32[]{:S(2)}) collective-permute-start(bf16[4,4,128,128]{3,2,1,0:T(8,128)(2,1)} %param.13), channel_id=1, source_target_pairs={{1,0},{2,1},{3,2},{4,3},{5,4},{6,5},{7,6},{8,7},{9,8},{10,9},{11,1... | collective-permute-start | bytes 1572872 | tf_op jit(solution)/shard_map/ppermute | solution.py:22
  10.7 0.8 copy.143
  11.4 0.8 copy.161
  12.2 0.8 broadcast_multiply_fusion
  13.2 0.6 gather_fusion.1
  13.8 0.6 gather_fusion.5
  14.4 0.6 gather_fusion.2
  15.0 0.1 copy.229
  15.1 0.6 gather_fusion.6
  15.7 0.1 copy.240
  15.8 0.1 copy.142
  15.9 0.1 copy.164
  16.2 0.6 gather_fusion.8
  16.8 0.1 copy.244
  17.0 0.1 copy.172
  17.2 0.1 copy.146
  17.6 0.1 fusion.97
  17.9 0.7 compare_and_fusion.6
  19.0 2.0 %copy.141 = bf16[4,4,128,128]{2,3,1,0:T(8,128)(2,1)} copy(bf16[4,4,128,128]{3,2,1,0:T(8,128)(2,1)} %param.13) | data formatting | bytes 1048576 | tf_op args[0]
  21.1 0.3 copy.157
  21.6 0.1 compare_reduce_fusion
  21.7 0.1 pad_maximum_fusion.6
  21.9 0.6 gather_fusion
  22.5 1.5 %fusion.92 = f32[4,4,128,128]{3,1,2,0:T(4,128)} fusion(bf16[4,3,128,128]{3,2,1,0:T(8,128)(2,1)S(1)} %bitcast.257, pred[4,3]{1,0:T(4,128)(4,1)S(1)} %get-tuple-element.24, s32[4,3]{1,0:T(4,128)S(1)} %copy-done.13), kind=kOutput, calls=%fused_computation.117 | convolution fusion | flops 1769520 | bytes 1441852 | tf_op jit(solution)/shard_map/rum,ruab->rmab/dot_general | solution.py:79
  24.0 1.6 %copy.159 = f32[4,4,128,128]{2,3,1,0:T(8,128)S(1)} copy(f32[4,4,128,128]{3,1,2,0:T(4,128)} %fusion.92) | data formatting | bytes 2097152 | tf_op jit(solution)/shard_map/rum,ruab->rmab/dot_general | solution.py:79
  25.7 0.1 fusion.79
  25.9 4.4 %collective-permute-start.7 = (bf16[4,4,128,128]{2,3,1,0:T(8,128)(2,1)S(1)}, bf16[4,4,128,128]{2,3,1,0:T(8,128)(2,1)}, u32[]{:S(2)}, u32[]{:S(2)}) collective-permute-start(bf16[4,4,128,128]{2,3,1,0:T(8,128)(2,1)S(1)} %fusion.79), channel_id=1, source_target_pairs={{1,0},{2,1},{3,2},{4,3},{5,4},{6,5},{7,6},{8,7},{9,8},{10,9},{11,1... | collective-permute-start | bytes 1572872 | tf_op jit(solution)/shard_map/ppermute | solution.py:22
  30.3 1.4 %pad_maximum_fusion = bf16[12,4,128,128]{3,2,1,0:T(8,128)(2,1)S(1)} fusion(bf16[4,4,128,128]{3,2,1,0:T(8,128)(2,1)} %collective-permute-done.1, bf16[4,4,128,128]{3,2,1,0:T(8,128)(2,1)S(1)} %copy-done.5, bf16[4,4,128,128]{3,2,1,0:T(8,128)(2,1)} %collective-permute-done), kind=kLoop, calls=%fused_computation.42 | loop fusion | flops 1572864 | bytes 3145728 | tf_op jit(solution)/shard_map/concatenate | solution.py:23
  31.7 2.1 %gather_fusion.3 = bf16[64,128,128]{2,1,0:T(8,128)(2,1)} fusion(bf16[48,128,128]{2,1,0:T(8,128)(2,1)S(1)} %bitcast.238, s32[1024]{0:T(1024)S(1)} %pad_clamp_fusion.4), kind=kCustom, calls=%fused_computation.2.clone | custom fusion | bytes 4194560 | tf_op jit(solution)/shard_map/jit(_take)/gather | solution.py:49
  33.8 3.5 %fusion.49 = bf16[4,4,128,128]{3,2,1,0:T(8,128)(2,1)} fusion(bf16[4,4,4,128,128]{4,3,2,1,0:T(8,128)(2,1)} %bitcast.249, pred[4,4,4]{2,1,0:T(4,128)(4,1)S(1)} %get-tuple-element.31, pred[4,4,4]{2,1,0:T(4,128)(4,1)S(1)} %compare_reduce_fusion.2, bf16[4,4,128,128]{3,2,1,0:T(8,128)(2,1)S(1)} %copy-done.5), kind=kOutput, calls=%fused_computation.77 | convolution fusion | flops 270794752 | bytes 3145856 | tf_op jit(solution)/shard_map/rkab,rknbc->rnac/dot_general | solution.py:51
  37.3 4.4 %collective-permute-start.9 = (bf16[4,4,128,128]{2,3,1,0:T(8,128)(2,1)}, bf16[4,4,128,128]{2,3,1,0:T(8,128)(2,1)}, u32[]{:S(2)}, u32[]{:S(2)}) collective-permute-start(bf16[4,4,128,128]{2,3,1,0:T(8,128)(2,1)} %bitcast.7), channel_id=1, source_target_pairs={{1,0},{2,1},{3,2},{4,3},{5,4},{6,5},{7,6},{8,7},{9,8},{10,9},{11,1... | collective-permute-start | bytes 1572872 | tf_op jit(solution)/shard_map/ppermute | solution.py:22
  41.8 2.1 %gather_fusion.9 = bf16[64,128,128]{2,1,0:T(8,128)(2,1)} fusion(bf16[48,128,128]{2,1,0:T(8,128)(2,1)S(1)} %bitcast.239, s32[1024]{0:T(1024)S(1)} %pad_clamp_fusion), kind=kCustom, calls=%fused_computation.8.clone | custom fusion | bytes 4194560 | tf_op jit(solution)/shard_map/jit(_take)/gather | solution.py:49
  43.9 3.9 %fusion.133 = (bf16[4,4,128,128]{2,3,1,0:T(8,128)(2,1)}, f32[4,4,128,128]{2,3,1,0:T(8,128)}) fusion(bf16[4,4,128,128]{3,2,1,0:T(8,128)(2,1)} %fusion.49, bf16[4,4,4,128,128]{4,3,2,1,0:T(8,128)(2,1)} %bitcast.250, pred[4,4,4]{2,1,0:T(4,128)(4,1)S(1)} %get-tuple-element.31, pred[4,4,4]{2,1,0:T(4,128)(4,1)S(1)} %compare_reduce_fusion.2, ...), kind=kOutput, calls=%fused_computation.205 | convolution fusion | flops 271843328 | bytes 4718720 | tf_op jit(solution)/shard_map/rkab,rknbc->rnac/dot_general | solution.py:51
  47.8 4.4 %collective-permute-start.3 = (bf16[4,4,128,128]{2,3,1,0:T(8,128)(2,1)}, bf16[4,4,128,128]{2,3,1,0:T(8,128)(2,1)}, u32[]{:S(2)}, u32[]{:S(2)}) collective-permute-start(bf16[4,4,128,128]{2,3,1,0:T(8,128)(2,1)} %get-tuple-element.37), channel_id=1, source_target_pairs={{1,0},{2,1},{3,2},{4,3},{5,4},{6,5},{7,6},{8,7},{9,8},{10,9},{11,1... | collective-permute-start | bytes 1572872 | tf_op jit(solution)/shard_map/ppermute | solution.py:22
  52.3 1.2 %pad_maximum_fusion.2 = bf16[12,4,128,128]{2,3,1,0:T(8,128)(2,1)S(1)} fusion(bf16[4,4,128,128]{2,3,1,0:T(8,128)(2,1)} %collective-permute-done.7, bf16[4,4,128,128]{2,3,1,0:T(8,128)(2,1)S(1)} %fusion.79, bf16[4,4,128,128]{2,3,1,0:T(8,128)(2,1)S(1)} %collective-permute-done.6), kind=kLoop, calls=%fused_computation.44 | loop fusion | flops 1572864 | bytes 3145728 | tf_op jit(solution)/shard_map/concatenate | solution.py:23
  53.5 0.9 copy.166
  54.4 2.1 %gather_fusion.7 = bf16[64,128,128]{2,1,0:T(8,128)(2,1)} fusion(bf16[48,128,128]{2,1,0:T(8,128)(2,1)S(1)} %copy.166, s32[1024]{0:T(1024)S(1)} %pad_clamp_fusion.2), kind=kCustom, calls=%fused_computation.7.clone | custom fusion | bytes 4194560 | tf_op jit(solution)/shard_map/jit(_take)/gather | solution.py:49
  56.5 3.9 %fusion.23 = f32[4,4,128,128]{3,2,1,0:T(8,128)} fusion(bf16[4,4,4,128,128]{4,3,2,1,0:T(8,128)(2,1)} %bitcast.255, pred[4,4,4]{2,1,0:T(4,128)(4,1)S(1)} %get-tuple-element.22, pred[4,4,4]{2,1,0:T(4,128)(4,1)S(1)} %get-tuple-element.14, bf16[4,4,128,128]{3,2,1,0:T(8,128)(2,1)} %fusion.49), kind=kOutput, calls=%fused_computation.51 | convolution fusion | flops 270532608 | bytes 3670144 | tf_op jit(solution)/shard_map/rkab,rknbc->rnac/dot_general | solution.py:51
  60.4 4.7 %fusion.35 = f32[4,4,128,128]{3,2,1,0:T(8,128)} fusion(f32[4,4,128,128]{3,2,1,0:T(8,128)} %fusion.23, bf16[4,4,4,128,128]{4,3,2,1,0:T(8,128)(2,1)S(1)} %bitcast.246, pred[4,4,4]{2,1,0:T(4,128)(4,1)S(1)} %get-tuple-element.17, pred[4,4,4]{2,1,0:T(4,128)(4,1)S(1)} %get-tuple-element.13, bf16[4,4,4,128,128]{4,3,2,1,0:T(8,128)(2,1)} %bitcast.256, ...), kind=kOutput, calls=%fused_computation.63 | convolution fusion | flops 541589504 | bytes 6816000 | tf_op jit(solution)/shard_map/rkab,rknbc->rnac/dot_general | solution.py:51
  65.0 1.5 %pad_maximum_fusion.3 = bf16[12,4,128,128]{2,3,1,0:T(8,128)(2,1)S(1)} fusion(bf16[4,4,128,128]{2,3,1,0:T(8,128)(2,1)} %collective-permute-done.9, bf16[4,4,128,128]{2,3,1,0:T(8,128)(2,1)} %bitcast.7, bf16[4,4,128,128]{2,3,1,0:T(8,128)(2,1)} %collective-permute-done.8), kind=kLoop, calls=%fused_computation.45 | loop fusion | flops 1572864 | bytes 3145728 | tf_op jit(solution)/shard_map/concatenate | solution.py:23
  66.6 0.9 copy.177
  67.5 2.1 %gather_fusion.10 = bf16[64,128,128]{2,1,0:T(8,128)(2,1)} fusion(bf16[48,128,128]{2,1,0:T(8,128)(2,1)S(1)} %copy.177, s32[1024]{0:T(1024)S(1)} %pad_clamp_fusion), kind=kCustom, calls=%fused_computation.9.clone | custom fusion | bytes 4194560 | tf_op jit(solution)/shard_map/jit(_take)/gather | solution.py:49
  69.7 4.3 %fusion.134 = (bf16[4,4,128,128]{2,3,1,0:T(8,128)(2,1)}, f32[4,4,128,128]{2,3,1,0:T(8,128)}) fusion(f32[4,4,128,128]{3,2,1,0:T(8,128)} %fusion.35, bf16[4,4,128,128]{2,3,1,0:T(8,128)(2,1)} %copy-done.9, bf16[4,4,4,128,128]{4,3,2,1,0:T(8,128)(2,1)} %bitcast.254, pred[4,4,4]{2,1,0:T(4,128)(4,1)S(1)} %get-tuple-element.17, ...), kind=kOutput, calls=%fused_computation.206 | convolution fusion | flops 272367616 | bytes 6815872 | tf_op jit(solution)/shard_map/rkab,rknbc->rnac/dot_general | solution.py:51
  74.0 4.4 %collective-permute-start.11 = (bf16[4,4,128,128]{2,3,1,0:T(8,128)(2,1)}, bf16[4,4,128,128]{2,3,1,0:T(8,128)(2,1)}, u32[]{:S(2)}, u32[]{:S(2)}) collective-permute-start(bf16[4,4,128,128]{2,3,1,0:T(8,128)(2,1)} %get-tuple-element.39), channel_id=1, source_target_pairs={{1,0},{2,1},{3,2},{4,3},{5,4},{6,5},{7,6},{8,7},{9,8},{10,9},{11,1... | collective-permute-start | bytes 1572872 | tf_op jit(solution)/shard_map/ppermute | solution.py:22
  78.4 1.5 %pad_maximum_fusion.1 = bf16[12,4,128,128]{2,3,1,0:T(8,128)(2,1)S(1)} fusion(bf16[4,4,128,128]{2,3,1,0:T(8,128)(2,1)} %collective-permute-done.3, bf16[4,4,128,128]{2,3,1,0:T(8,128)(2,1)} %get-tuple-element.37, bf16[4,4,128,128]{2,3,1,0:T(8,128)(2,1)} %collective-permute-done.2), kind=kLoop, calls=%fused_computation.43 | loop fusion | flops 1572864 | bytes 3145728 | tf_op jit(solution)/shard_map/concatenate | solution.py:23
  79.9 0.9 copy.152
  80.9 2.1 %gather_fusion.4 = bf16[64,128,128]{2,1,0:T(8,128)(2,1)} fusion(bf16[48,128,128]{2,1,0:T(8,128)(2,1)S(1)} %copy.152, s32[1024]{0:T(1024)S(1)} %pad_clamp_fusion.4), kind=kCustom, calls=%fused_computation.6.clone | custom fusion | bytes 4194560 | tf_op jit(solution)/shard_map/jit(_take)/gather | solution.py:49
  83.0 3.7 %fusion.50 = bf16[4,4,128,128]{3,2,1,0:T(8,128)(2,1)} fusion(bf16[4,4,4,128,128]{4,3,2,1,0:T(8,128)(2,1)} %bitcast.251, pred[4,4,4]{2,1,0:T(4,128)(4,1)S(1)} %get-tuple-element.31, pred[4,4,4]{2,1,0:T(4,128)(4,1)S(1)} %compare_reduce_fusion.2, bf16[4,4,128,128]{2,3,1,0:T(8,128)(2,1)} %get-tuple-element.37), kind=kOutput, calls=%fused_computation.78 | convolution fusion | flops 270794752 | bytes 3145856 | tf_op jit(solution)/shard_map/rkab,rknbc->rnac/dot_general | solution.py:51
  86.7 4.4 %collective-permute-start.13 = (bf16[4,4,128,128]{2,3,1,0:T(8,128)(2,1)}, bf16[4,4,128,128]{2,3,1,0:T(8,128)(2,1)}, u32[]{:S(2)}, u32[]{:S(2)}) collective-permute-start(bf16[4,4,128,128]{2,3,1,0:T(8,128)(2,1)} %bitcast.17), channel_id=1, source_target_pairs={{1,0},{2,1},{3,2},{4,3},{5,4},{6,5},{7,6},{8,7},{9,8},{10,9},{11,1... | collective-permute-start | bytes 1572872 | tf_op jit(solution)/shard_map/ppermute | solution.py:22
  91.1 2.2 %fusion.41 = f32[4,4,128,128]{2,3,1,0:T(8,128)S(1)} fusion(bf16[4,4,4,128,128]{4,3,2,1,0:T(8,128)(2,1)S(1)} %bitcast.252, pred[4,4,4]{2,1,0:T(4,128)(4,1)S(1)} %get-tuple-element.31, pred[4,4,4]{2,1,0:T(4,128)(4,1)S(1)} %compare_reduce_fusion.2, f32[4,4,128,128]{2,3,1,0:T(8,128)S(1)} %copy-done.14, bf16[4,4,128,128]{3,2,1,0:T(8,128)(2,1)} %fusion.50), kind=kOutput, calls=%fused_computation.69 | convolution fusion | flops 271581184 | bytes 4718720 | tf_op jit(solution)/shard_map/rkab,rknbc->rnac/dot_general | solution.py:51
  93.3 2.1 %gather_fusion.12 = bf16[64,128,128]{2,1,0:T(8,128)(2,1)} fusion(bf16[48,128,128]{2,1,0:T(8,128)(2,1)S(1)} %copy.152, s32[1024]{0:T(1024)S(1)} %pad_clamp_fusion), kind=kCustom, calls=%fused_computation.11.clone | custom fusion | bytes 4194560 | tf_op jit(solution)/shard_map/jit(_take)/gather | solution.py:49
  95.5 1.3 %copy.191 = f32[4,4,128,128]{3,2,1,0:T(8,128)} copy(f32[4,4,128,128]{2,3,1,0:T(8,128)S(1)} %fusion.41) | data formatting | bytes 2097152
  96.8 1.5 %pad_maximum_fusion.4 = bf16[12,4,128,128]{2,3,1,0:T(8,128)(2,1)S(1)} fusion(bf16[4,4,128,128]{2,3,1,0:T(8,128)(2,1)} %collective-permute-done.11, bf16[4,4,128,128]{2,3,1,0:T(8,128)(2,1)} %get-tuple-element.39, bf16[4,4,128,128]{2,3,1,0:T(8,128)(2,1)} %collective-permute-done.10), kind=kLoop, calls=%fused_computation.46 | loop fusion | flops 1572864 | bytes 3145728 | tf_op jit(solution)/shard_map/concatenate | solution.py:23
  98.3 0.9 copy.180
  99.2 2.1 %gather_fusion.11 = bf16[64,128,128]{2,1,0:T(8,128)(2,1)} fusion(bf16[48,128,128]{2,1,0:T(8,128)(2,1)S(1)} %copy.180, s32[1024]{0:T(1024)S(1)} %pad_clamp_fusion.2), kind=kCustom, calls=%fused_computation.10.clone | custom fusion | bytes 4194560 | tf_op jit(solution)/shard_map/jit(_take)/gather | solution.py:49
  101.4 3.7 %fusion.21 = f32[4,4,128,128]{3,2,1,0:T(8,128)} fusion(bf16[4,4,4,128,128]{4,3,2,1,0:T(8,128)(2,1)} %bitcast.247, pred[4,4,4]{2,1,0:T(4,128)(4,1)S(1)} %get-tuple-element.22, pred[4,4,4]{2,1,0:T(4,128)(4,1)S(1)} %get-tuple-element.14, bf16[4,4,128,128]{3,2,1,0:T(8,128)(2,1)} %fusion.50), kind=kOutput, calls=%fused_computation.49 | convolution fusion | flops 270532608 | bytes 3670144 | tf_op jit(solution)/shard_map/rkab,rknbc->rnac/dot_general | solution.py:51
  105.1 1.5 %pad_maximum_fusion.5 = bf16[12,4,128,128]{2,3,1,0:T(8,128)(2,1)S(1)} fusion(bf16[4,4,128,128]{2,3,1,0:T(8,128)(2,1)} %collective-permute-done.13, bf16[4,4,128,128]{2,3,1,0:T(8,128)(2,1)} %bitcast.17, bf16[4,4,128,128]{2,3,1,0:T(8,128)(2,1)} %collective-permute-done.12), kind=kLoop, calls=%fused_computation.47 | loop fusion | flops 1572864 | bytes 3145728 | tf_op jit(solution)/shard_map/concatenate | solution.py:23
  106.6 0.9 copy.188
  107.5 2.2 %gather_fusion.13 = bf16[64,128,128]{2,1,0:T(8,128)(2,1)} fusion(bf16[48,128,128]{2,1,0:T(8,128)(2,1)S(1)} %copy.188, s32[1024]{0:T(1024)S(1)} %pad_clamp_fusion), kind=kCustom, calls=%fused_computation.12.clone | custom fusion | bytes 4194560 | tf_op jit(solution)/shard_map/jit(_take)/gather | solution.py:49
  109.7 5.6 %fusion.33 = f32[4,4,128,128]{3,2,1,0:T(8,128)} fusion(f32[4,4,128,128]{3,2,1,0:T(8,128)} %fusion.21, bf16[4,4,4,128,128]{4,3,2,1,0:T(8,128)(2,1)} %bitcast.245, pred[4,4,4]{2,1,0:T(4,128)(4,1)S(1)} %get-tuple-element.17, pred[4,4,4]{2,1,0:T(4,128)(4,1)S(1)} %get-tuple-element.13, bf16[4,4,4,128,128]{4,3,2,1,0:T(8,128)(2,1)} %bitcast.248, ...), kind=kOutput, calls=%fused_computation.61 | convolution fusion | flops 541589504 | bytes 6816000 | tf_op jit(solution)/shard_map/rkab,rknbc->rnac/dot_general | solution.py:51
  115.3 2.8 %fusion.48 = f32[4,4,128,128]{2,3,1,0:T(8,128)S(1)} fusion(f32[4,4,128,128]{3,2,1,0:T(8,128)} %fusion.33, bf16[4,4,4,128,128]{4,3,2,1,0:T(8,128)(2,1)S(1)} %bitcast.253, pred[4,4,4]{2,1,0:T(4,128)(4,1)S(1)} %get-tuple-element.17, pred[4,4,4]{2,1,0:T(4,128)(4,1)S(1)} %get-tuple-element.13, f32[4,4,128,128]{2,3,1,0:T(8,128)} %get-tuple-element.40, ...), kind=kOutput, calls=%fused_computation.76 | convolution fusion | flops 271581184 | bytes 5767296 | tf_op jit(solution)/shard_map/rkab,rknbc->rnac/dot_general | solution.py:51
  118.0 1.3 %copy.192 = f32[4,4,128,128]{3,2,1,0:T(8,128)} copy(f32[4,4,128,128]{2,3,1,0:T(8,128)S(1)} %fusion.48) | data formatting | bytes 2097152
  (83 shorter events, 1.9 us)
Async XLA Ops:
  0.6 21.1 %copy-start.12 = (bf16[12,128,128]{2,1,0:T(8,128)(2,1)S(1)}, bf16[12,128,128]{2,1,0:T(8,128)(2,1)}, u32[]{:S(2)}) copy-start(bf16[12,128,128]{2,1,0:T(8,128)(2,1)} %param.17) | copy-start | bytes 1179652
  0.6 20.4 %copy-start.10 = (bf16[4,4,128,128]{3,2,1,0:T(8,128)(2,1)S(1)}, bf16[4,4,128,128]{3,2,1,0:T(8,128)(2,1)}, u32[]{:S(2)}) copy-start(bf16[4,4,128,128]{3,2,1,0:T(8,128)(2,1)} %param.15) | copy-start | bytes 1572868
  0.6 21.1 %collective-permute-start.4 = (bf16[12,128,128]{2,1,0:T(8,128)(2,1)}, bf16[12,128,128]{2,1,0:T(8,128)(2,1)S(1)}, u32[]{:S(2)}, u32[]{:S(2)}) collective-permute-start(bf16[12,128,128]{2,1,0:T(8,128)(2,1)} %param.17), channel_id=1, source_target_pairs={{0,1},{1,2},{2,3},{3,4},{4,5},{5,6},{6,7},{7,8},{8,9},{9,10},{10,1... | collective-permute-start | bytes 1179656 | tf_op jit(solution)/shard_map/ppermute | solution.py:30
  1.2 20.6 %collective-permute-start.5 = (bf16[12,128,128]{2,1,0:T(8,128)(2,1)}, bf16[12,128,128]{2,1,0:T(8,128)(2,1)S(1)}, u32[]{:S(2)}, u32[]{:S(2)}) collective-permute-start(bf16[12,128,128]{2,1,0:T(8,128)(2,1)} %param.17), channel_id=1, source_target_pairs={{0,15},{1,0},{2,1},{3,2},{4,3},{5,4},{6,5},{7,6},{8,7},{9,8},{10,9... | collective-permute-start | bytes 1179656 | tf_op jit(solution)/shard_map/ppermute | solution.py:30
  6.2 24.1 %collective-permute-start = (bf16[4,4,128,128]{3,2,1,0:T(8,128)(2,1)}, bf16[4,4,128,128]{3,2,1,0:T(8,128)(2,1)}, u32[]{:S(2)}, u32[]{:S(2)}) collective-permute-start(bf16[4,4,128,128]{3,2,1,0:T(8,128)(2,1)} %param.13), channel_id=1, source_target_pairs={{0,1},{1,2},{2,3},{3,4},{4,5},{5,6},{6,7},{7,8},{8,9},{9,10},{10,1... | collective-permute-start | bytes 1572872 | tf_op jit(solution)/shard_map/ppermute | solution.py:21
  6.2 24.1 %collective-permute-start.1 = (bf16[4,4,128,128]{3,2,1,0:T(8,128)(2,1)}, bf16[4,4,128,128]{3,2,1,0:T(8,128)(2,1)}, u32[]{:S(2)}, u32[]{:S(2)}) collective-permute-start(bf16[4,4,128,128]{3,2,1,0:T(8,128)(2,1)} %param.13), channel_id=1, source_target_pairs={{1,0},{2,1},{3,2},{4,3},{5,4},{6,5},{7,6},{8,7},{9,8},{10,9},{11,1... | collective-permute-start | bytes 1572872 | tf_op jit(solution)/shard_map/ppermute | solution.py:22
  21.1 1.4 %copy-start.13 = (s32[4,3]{1,0:T(4,128)S(1)}, s32[4,3]{1,0:T(4,128)}, u32[]{:S(2)}) copy-start(s32[4,3]{1,0:T(4,128)} %param.19) | copy-start | bytes 148
  21.4 4.3 %copy-start.7 = (bf16[4,4,128,128]{2,3,1,0:T(8,128)(2,1)}, bf16[4,4,128,128]{2,3,1,0:T(8,128)(2,1)S(1)}, u32[]{:S(2)}) copy-start(bf16[4,4,128,128]{2,3,1,0:T(8,128)(2,1)S(1)} %copy.157) | copy-start | bytes 1572868
  24.0 6.3 %copy-start.5 = (bf16[4,4,128,128]{3,2,1,0:T(8,128)(2,1)S(1)}, bf16[4,4,128,128]{3,2,1,0:T(8,128)(2,1)}, u32[]{:S(2)}) copy-start(bf16[4,4,128,128]{3,2,1,0:T(8,128)(2,1)} %param.13) | copy-start | bytes 1572868
  25.6 4.7 %copy-start = (f32[4,4,128,128]{2,3,1,0:T(8,128)}, f32[4,4,128,128]{2,3,1,0:T(8,128)S(1)}, u32[]{:S(2)}) copy-start(f32[4,4,128,128]{2,3,1,0:T(8,128)S(1)} %copy.159) | copy-start | bytes 3145732
  25.8 26.5 %copy-start.9 = (bf16[4,4,128,128]{2,3,1,0:T(8,128)(2,1)}, bf16[4,4,128,128]{2,3,1,0:T(8,128)(2,1)S(1)}, u32[]{:S(2)}) copy-start(bf16[4,4,128,128]{2,3,1,0:T(8,128)(2,1)S(1)} %fusion.79) | copy-start | bytes 1572868
  25.8 22.0 %collective-permute-start.6 = (bf16[4,4,128,128]{2,3,1,0:T(8,128)(2,1)S(1)}, bf16[4,4,128,128]{2,3,1,0:T(8,128)(2,1)S(1)}, u32[]{:S(2)}, u32[]{:S(2)}) collective-permute-start(bf16[4,4,128,128]{2,3,1,0:T(8,128)(2,1)S(1)} %fusion.79), channel_id=1, source_target_pairs={{0,1},{1,2},{2,3},{3,4},{4,5},{5,6},{6,7},{7,8},{8,9},{9,10},{10,1... | collective-permute-start | bytes 1572872 | tf_op jit(solution)/shard_map/ppermute | solution.py:21
  25.9 26.4 %collective-permute-start.7 = (bf16[4,4,128,128]{2,3,1,0:T(8,128)(2,1)S(1)}, bf16[4,4,128,128]{2,3,1,0:T(8,128)(2,1)}, u32[]{:S(2)}, u32[]{:S(2)}) collective-permute-start(bf16[4,4,128,128]{2,3,1,0:T(8,128)(2,1)S(1)} %fusion.79), channel_id=1, source_target_pairs={{1,0},{2,1},{3,2},{4,3},{5,4},{6,5},{7,6},{8,7},{9,8},{10,9},{11,1... | collective-permute-start | bytes 1572872 | tf_op jit(solution)/shard_map/ppermute | solution.py:22
  37.3 6.6 %copy-start.11 = (bf16[4,4,128,128]{2,3,1,0:T(8,128)(2,1)S(1)}, bf16[4,4,128,128]{2,3,1,0:T(8,128)(2,1)}, u32[]{:S(2)}) copy-start(bf16[4,4,128,128]{2,3,1,0:T(8,128)(2,1)} %copy.141) | copy-start | bytes 1572868
  37.3 27.7 %collective-permute-start.8 = (bf16[4,4,128,128]{2,3,1,0:T(8,128)(2,1)}, bf16[4,4,128,128]{2,3,1,0:T(8,128)(2,1)}, u32[]{:S(2)}, u32[]{:S(2)}) collective-permute-start(bf16[4,4,128,128]{2,3,1,0:T(8,128)(2,1)} %bitcast.7), channel_id=1, source_target_pairs={{0,1},{1,2},{2,3},{3,4},{4,5},{5,6},{6,7},{7,8},{8,9},{9,10},{10,1... | collective-permute-start | bytes 1572872 | tf_op jit(solution)/shard_map/ppermute | solution.py:21
  37.3 27.7 %collective-permute-start.9 = (bf16[4,4,128,128]{2,3,1,0:T(8,128)(2,1)}, bf16[4,4,128,128]{2,3,1,0:T(8,128)(2,1)}, u32[]{:S(2)}, u32[]{:S(2)}) collective-permute-start(bf16[4,4,128,128]{2,3,1,0:T(8,128)(2,1)} %bitcast.7), channel_id=1, source_target_pairs={{1,0},{2,1},{3,2},{4,3},{5,4},{6,5},{7,6},{8,7},{9,8},{10,9},{11,1... | collective-permute-start | bytes 1572872 | tf_op jit(solution)/shard_map/ppermute | solution.py:22
  47.8 30.6 %collective-permute-start.2 = (bf16[4,4,128,128]{2,3,1,0:T(8,128)(2,1)}, bf16[4,4,128,128]{2,3,1,0:T(8,128)(2,1)}, u32[]{:S(2)}, u32[]{:S(2)}) collective-permute-start(bf16[4,4,128,128]{2,3,1,0:T(8,128)(2,1)} %get-tuple-element.37), channel_id=1, source_target_pairs={{0,1},{1,2},{2,3},{3,4},{4,5},{5,6},{6,7},{7,8},{8,9},{9,10},{10,1... | collective-permute-start | bytes 1572872 | tf_op jit(solution)/shard_map/ppermute | solution.py:21
  47.8 30.6 %collective-permute-start.3 = (bf16[4,4,128,128]{2,3,1,0:T(8,128)(2,1)}, bf16[4,4,128,128]{2,3,1,0:T(8,128)(2,1)}, u32[]{:S(2)}, u32[]{:S(2)}) collective-permute-start(bf16[4,4,128,128]{2,3,1,0:T(8,128)(2,1)} %get-tuple-element.37), channel_id=1, source_target_pairs={{1,0},{2,1},{3,2},{4,3},{5,4},{6,5},{7,6},{8,7},{9,8},{10,9},{11,1... | collective-permute-start | bytes 1572872 | tf_op jit(solution)/shard_map/ppermute | solution.py:22
  56.5 3.9 %copy-start.2 = (bf16[64,128,128]{2,1,0:T(8,128)(2,1)S(1)}, bf16[64,128,128]{2,1,0:T(8,128)(2,1)}, u32[]{:S(2)}) copy-start(bf16[64,128,128]{2,1,0:T(8,128)(2,1)} %gather_fusion.9) | copy-start | bytes 6291460
  56.5 3.9 %copy-start.6 = (bf16[4,4,128,128]{3,2,1,0:T(8,128)(2,1)S(1)}, bf16[4,4,128,128]{3,2,1,0:T(8,128)(2,1)}, u32[]{:S(2)}) copy-start(bf16[4,4,128,128]{3,2,1,0:T(8,128)(2,1)} %param.13) | copy-start | bytes 1572868
  67.5 2.2 %copy-start.1 = (f32[4,4,128,128]{2,3,1,0:T(8,128)S(1)}, f32[4,4,128,128]{2,3,1,0:T(8,128)}, u32[]{:S(2)}) copy-start(f32[4,4,128,128]{2,3,1,0:T(8,128)} %copy-done) | copy-start | bytes 3145732
  67.5 2.2 %copy-start.8 = (bf16[4,4,128,128]{2,3,1,0:T(8,128)(2,1)S(1)}, bf16[4,4,128,128]{2,3,1,0:T(8,128)(2,1)}, u32[]{:S(2)}) copy-start(bf16[4,4,128,128]{2,3,1,0:T(8,128)(2,1)} %copy-done.7) | copy-start | bytes 1572868
  74.0 22.8 %collective-permute-start.10 = (bf16[4,4,128,128]{2,3,1,0:T(8,128)(2,1)}, bf16[4,4,128,128]{2,3,1,0:T(8,128)(2,1)}, u32[]{:S(2)}, u32[]{:S(2)}) collective-permute-start(bf16[4,4,128,128]{2,3,1,0:T(8,128)(2,1)} %get-tuple-element.39), channel_id=1, source_target_pairs={{0,1},{1,2},{2,3},{3,4},{4,5},{5,6},{6,7},{7,8},{8,9},{9,10},{10,1... | collective-permute-start | bytes 1572872 | tf_op jit(solution)/shard_map/ppermute | solution.py:21
  74.0 22.8 %collective-permute-start.11 = (bf16[4,4,128,128]{2,3,1,0:T(8,128)(2,1)}, bf16[4,4,128,128]{2,3,1,0:T(8,128)(2,1)}, u32[]{:S(2)}, u32[]{:S(2)}) collective-permute-start(bf16[4,4,128,128]{2,3,1,0:T(8,128)(2,1)} %get-tuple-element.39), channel_id=1, source_target_pairs={{1,0},{2,1},{3,2},{4,3},{5,4},{6,5},{7,6},{8,7},{9,8},{10,9},{11,1... | collective-permute-start | bytes 1572872 | tf_op jit(solution)/shard_map/ppermute | solution.py:22
  83.0 8.1 %copy-start.3 = (bf16[64,128,128]{2,1,0:T(8,128)(2,1)S(1)}, bf16[64,128,128]{2,1,0:T(8,128)(2,1)}, u32[]{:S(2)}) copy-start(bf16[64,128,128]{2,1,0:T(8,128)(2,1)} %gather_fusion.4) | copy-start | bytes 6291460
  83.0 8.1 %copy-start.14 = (f32[4,4,128,128]{2,3,1,0:T(8,128)S(1)}, f32[4,4,128,128]{2,3,1,0:T(8,128)}, u32[]{:S(2)}) copy-start(f32[4,4,128,128]{2,3,1,0:T(8,128)} %get-tuple-element.38) | copy-start | bytes 3145732
  86.7 18.4 %collective-permute-start.12 = (bf16[4,4,128,128]{2,3,1,0:T(8,128)(2,1)}, bf16[4,4,128,128]{2,3,1,0:T(8,128)(2,1)}, u32[]{:S(2)}, u32[]{:S(2)}) collective-permute-start(bf16[4,4,128,128]{2,3,1,0:T(8,128)(2,1)} %bitcast.17), channel_id=1, source_target_pairs={{0,1},{1,2},{2,3},{3,4},{4,5},{5,6},{6,7},{7,8},{8,9},{9,10},{10,1... | collective-permute-start | bytes 1572872 | tf_op jit(solution)/shard_map/ppermute | solution.py:21
  86.7 18.4 %collective-permute-start.13 = (bf16[4,4,128,128]{2,3,1,0:T(8,128)(2,1)}, bf16[4,4,128,128]{2,3,1,0:T(8,128)(2,1)}, u32[]{:S(2)}, u32[]{:S(2)}) collective-permute-start(bf16[4,4,128,128]{2,3,1,0:T(8,128)(2,1)} %bitcast.17), channel_id=1, source_target_pairs={{1,0},{2,1},{3,2},{4,3},{5,4},{6,5},{7,6},{8,7},{9,8},{10,9},{11,1... | collective-permute-start | bytes 1572872 | tf_op jit(solution)/shard_map/ppermute | solution.py:22
  109.7 5.6 %copy-start.4 = (bf16[64,128,128]{2,1,0:T(8,128)(2,1)S(1)}, bf16[64,128,128]{2,1,0:T(8,128)(2,1)}, u32[]{:S(2)}) copy-start(bf16[64,128,128]{2,1,0:T(8,128)(2,1)} %gather_fusion.13) | copy-start | bytes 6291460
where the time goes:
time: 120 us; the launch traced here: 119 us
  matrix products  39.6 us (33%)
  local copies, waits for them, and re-layouts  35.2 us (29%)
  starting transfers between devices  32.2 us (27%)
  other arithmetic  11.3 us (9%)
    dot_general x10, matrix products, multiply(): jnp.einsum('rkab,rknbc->rnac', left_blocks, picked, preferred_element_typ...  38.1 us
    ppermute x6, starting transfers between devices, with_halo(): after = lax.ppermute(leading, axis, down)  26.6 us
    gather x8, local copies, waits for them, and re-layouts, multiply(): jnp.take(right_wide.reshape(-1, block_size, block_size), flat_pos, axis=0)  17.1 us
    concatenate x6, other arithmetic, with_halo(): shard = jnp.concatenate([before, shard, after], axis=dim)  8.71 us
    unnamed x36, local copies, waits for them, and re-layouts  6.54 us
    ppermute x2, starting transfers between devices, shifted(): return lax.ppermute(value, axis, pairs)  5.53 us
    reshape x5, local copies, waits for them, and re-layouts, multiply(): right_wide.reshape(-1, block_size, block_size)  4.52 us
  transfers between devices with their start and end apart: 14, of which 0 were waited for; matrix products, arithmetic and copies ran while one was open for 60% of the time, Pallas kernels for 0%

commit v1 on v0

v1 whole, which is shorter than its diff:
```python
import functools
import math

import jax
import jax.numpy as jnp
from jax import lax
from jax.experimental import pallas as pl
from jax.experimental.pallas import tpu as pltpu
from jax.sharding import PartitionSpec as P

BLK = 128
REACH = 4
KB = 4
KD = 3
F32 = jnp.float32
BF16 = jnp.bfloat16
MESH = pl.DeviceIdType.MESH
VMEM_BYTES = 40 * 1024 * 1024


def kernel(
    total_rows,
    devices,
    e_cols,
    p1_cols,
    dh_source,
    dh_slot,
    source_hbm,
    e_hbm,
    p1_hbm,
    dh_hbm,
    e_out,
    p1_out,
    dev_wide,
    resp_wide,
    square_wide,
    next_wide,
    next_square,
    next_resp,
    left_prod,
    resp_f32,
    next_f32,
    p1_own,
    dh_own,
    dh_near,
    stage,
    source_vmem,
    source_smem,
    table,
    e_stage,
    p1_stage,
    local_sem,
    send_sem,
    recv_sem,
):
    rows = REACH
    own = rows * KB
    owned = rows * KD
    me = lax.axis_index("row")
    above = lax.rem(me + 1, devices)
    below = lax.rem(me + devices - 1, devices)
    row_start = me * rows

    def local(src, dst, sem):
        return pltpu.make_async_copy(src, dst, local_sem.at[sem])

    def remote(src, dst, sem, target):
        return pltpu.make_async_remote_copy(
            src_ref=src,
            dst_ref=dst,
            send_sem=send_sem.at[sem],
            recv_sem=recv_sem.at[sem],
            device_id={"row": target},
            device_id_type=MESH,
        )

    get_e = local(e_hbm, dev_wide.at[pl.ds(2 * own, own)], 0)
    get_p1 = local(p1_hbm, p1_own, 1)
    get_dh = local(dh_hbm, dh_own, 2)
    get_near = local(dh_hbm, dh_near.at[pl.ds(4, owned)], 3)
    get_e.start()
    get_dh.start()
    get_p1.start()
    get_near.start()

    barrier = pltpu.get_barrier_semaphore()
    for neighbour in (below, above):
        pl.semaphore_signal(
            barrier, inc=1, device_id={"row": neighbour}, device_id_type=MESH
        )
    pl.semaphore_wait(barrier, 2)

    src_up = remote(source_hbm, source_vmem.at[0], 0, above)
    src_down = remote(source_hbm, source_vmem.at[1], 1, below)
    src_up.start()
    src_down.start()
    dev_up = remote(e_hbm, dev_wide.at[pl.ds(own, own)], 2, above)
    dev_down = remote(e_hbm, dev_wide.at[pl.ds(3 * own, own)], 3, below)
    dev_up.start()
    dev_down.start()

    zero = jnp.zeros((BLK, BLK), BF16)
    dev_wide[4 * own] = zero
    for ref in (resp_wide, square_wide, next_wide, next_square, next_resp):
        ref[3 * own] = zero
    dh_near[owned + 8] = zero

    src_up.wait()
    src_down.wait()
    for side in range(2):
        to_smem = local(source_vmem.at[side], source_smem.at[side], 4 + side)
        to_smem.start()
        to_smem.wait()
    get_dh.wait()

    def fill_stage(side):
        count = jnp.int32(0)
        picked = [jnp.int32(0)] * 4
        for row in range(rows):
            for u in range(KD):
                position = source_smem[side, row, u]
                mine = lax.div(position, owned) == me
                here = position - me * owned
                for slot in range(4):
                    hit = jnp.logical_and(mine, count == slot)
                    picked[slot] = jnp.where(hit, here, picked[slot])
                count = count + jnp.where(mine, 1, 0)
        for slot in range(4):
            stage[side, slot] = dh_own[picked[slot]]

    fill_stage(0)
    fill_stage(1)
    dh_down = remote(stage.at[0], dh_near.at[pl.ds(owned + 4, 4)], 4, below)
    dh_up = remote(stage.at[1], dh_near.at[pl.ds(0, 4)], 5, above)
    dh_down.start()
    dh_up.start()

    def fill(base, first_row, left, right, target, low, high):
        def one(i, carry):
            row = lax.rem(row_start + first_row + i + total_rows, total_rows)
            wanted = [target[row, n] for n in range(KB)]
            for k in range(KB):
                col = left[row, k]
                near = lax.rem(col - row_start + 2 * REACH + total_rows, total_rows)
                start = near * KB + jnp.where(near >= 4 * REACH, 1, 0)
                held = [right[col, m] for m in range(KB)]
                for n in range(KB):
                    at = jnp.int32(4 * own)
                    for m in range(KB):
                        at = jnp.where(held[m] == wanted[n], start + m, at)
                    table[base + i * KB * KB + k * KB + n] = jnp.clip(at, low, high)
            return carry

        return one

    ee, ee_own, ep, pe = (rows_before * KB * KB for rows_before in (0, 12, 16, 20))
    lax.fori_loop(0, 12, fill(ee, -REACH, e_cols, e_cols, e_cols, 0, 5 * own), 0)
    for base, left, right, target in (
        (ee_own, e_cols, e_cols, e_cols),
        (ep, e_cols, p1_cols, p1_cols),
        (pe, p1_cols, e_cols, p1_cols),
    ):
        lax.fori_loop(0, 4, fill(base, 0, left, right, target, own, 4 * own), 0)

    dev_up.wait()
    dev_down.wait()
    fwd_up = remote(
        dev_wide.at[pl.ds(own, own)], dev_wide.at[pl.ds(0, own)], 6, above
    )
    fwd_down = remote(
        dev_wide.at[pl.ds(3 * own, own)], dev_wide.at[pl.ds(4 * own + 1, own)], 7, below
    )
    fwd_up.start()
    fwd_down.start()

    get_p1.wait()
    get_near.wait()
    dh_down.wait()
    dh_up.wait()
    from_below, from_above = jnp.int32(0), jnp.int32(0)
    for row in range(rows):
        at = [jnp.int32(owned + 8)] * KB
        for u in range(KD):
            position = dh_source[row, u]
            owner = lax.div(position, owned)
            is_below, is_above = owner == below, owner == above
            place = jnp.where(
                is_below,
                from_below,
                jnp.where(is_above, owned + 4 + from_above, 4 + position - me * owned),
            )
            place = jnp.clip(place, 0, owned + 8)
            from_below = from_below + jnp.where(is_below, 1, 0)
            from_above = from_above + jnp.where(is_above, 1, 0)
            slot = dh_slot[row, u]
            for m in range(KB):
                at[m] = jnp.where(slot == m, place, at[m])
        for m in range(KB):
            q = row * KB + m
            value = p1_own[q].astype(F32) + dh_near[at[m]].astype(F32)
            resp_f32[q] = value
            resp_wide[own + q] = value.astype(BF16)
    resp_up = remote(resp_wide.at[pl.ds(own, own)], resp_wide.at[pl.ds(0, own)], 8, above)
    resp_down = remote(
        resp_wide.at[pl.ds(own, own)], resp_wide.at[pl.ds(2 * own, own)], 9, below
    )
    resp_up.start()
    resp_down.start()

    def product(i, terms, sink):
        for pair in range(KB // 2):
            acc = None
            for left, left_base, right, right_off, base in terms:
                for half in range(KB // 2):
                    ks = (2 * half, 2 * half + 1)
                    ns = (2 * pair, 2 * pair + 1)
                    a = jnp.concatenate([left[left_base + i * KB + k] for k in ks], axis=1)
                    b = jnp.concatenate(
                        [
                            jnp.concatenate(
                                [
                                    right[table[base + i * KB * KB + k * KB + n] - right_off]
                                    for n in ns
                                ],
                                axis=1,
                            )
                            for k in ks
                        ],
                        axis=0,
                    )
                    part = jnp.dot(a, b, preferred_element_type=F32)
                    acc = part if acc is None else acc + part
            for j in range(2):
                sink(i * KB + 2 * pair + j, acc[:, j * BLK : (j + 1) * BLK])

    def run(count, terms, sink):
        def one(i, carry):
            product(i, terms, sink)
            return carry

        lax.fori_loop(0, count, one, 0)

    get_e.wait()
    fwd_up.wait()
    fwd_down.wait()

    def to_square(q, value):
        square_wide[q] = value.astype(BF16)

    run(12, [(dev_wide, own, dev_wide, 0, ee)], to_square)

    def to_next(q, value):
        new = 1.5 * dev_wide[own + q].astype(F32) - 2.0 * value
        next_f32[q] = new
        next_wide[q] = new.astype(BF16)

    run(12, [(square_wide, 0, dev_wide, 0, ee)], to_next)

    def to_next_square(q, value):
        next_square[own + q] = value.astype(BF16)

    run(4, [(next_wide, own, next_wide, own, ee_own)], to_next_square)
    sq_up = remote(
        next_square.at[pl.ds(own, own)], next_square.at[pl.ds(0, own)], 10, above
    )
    sq_down = remote(
        next_square.at[pl.ds(own, own)], next_square.at[pl.ds(2 * own, own)], 11, below
    )
    sq_up.start()
    sq_down.start()

    resp_up.wait()
    resp_down.wait()

    def to_left(q, value):
        left_prod[q] = value.astype(BF16)

    run(4, [(dev_wide, 2 * own, resp_wide, own, ep)], to_left)

    def to_resp(q, value):
        new = 1.5 * resp_f32[q] - 2.0 * value
        resp_f32[q] = new
        next_resp[own + q] = new.astype(BF16)

    run(
        4,
        [
            (square_wide, own, resp_wide, own, ep),
            (left_prod, 0, dev_wide, 0, pe),
            (resp_wide, own, square_wide, own, pe),
        ],
        to_resp,
    )
    next_up = remote(next_resp.at[pl.ds(own, own)], next_resp.at[pl.ds(0, own)], 12, above)
    next_down = remote(
        next_resp.at[pl.ds(own, own)], next_resp.at[pl.ds(2 * own, own)], 13, below
    )
    next_up.start()
    next_down.start()

    def to_e(q, value):
        e_stage[q] = 1.5 * next_f32[own + q] - 2.0 * value

    run(4, [(next_square, own, next_wide, own, ee_own)], to_e)
    put_e = local(e_stage, e_out, 6)
    put_e.start()

    sq_up.wait()
    sq_down.wait()

    def to_back(q, value):
        resp_f32[q] = 1.5 * resp_f32[q] - 2.0 * value

    run(4, [(next_resp, own, next_square, own, pe)], to_back)

    next_up.wait()
    next_down.wait()
    run(4, [(next_wide, own, next_resp, own, ep)], to_left)

    def to_out(q, value):
        p1_stage[q] = 0.5 * resp_f32[q] - value

    run(
        4,
        [(next_square, own, next_resp, own, ep), (left_prod, 0, next_wide, own, pe)],
        to_out,
    )
    put_p1 = local(p1_stage, p1_out, 7)
    put_p1.start()
    put_e.wait()
    put_p1.wait()


def body(e_blocks, e_cols, p1_blocks, p1_cols, dh_owned, dh_source, dh_slot):
    rows, slots, blk = e_blocks.shape[:3]
    own = rows * slots
    owned = dh_owned.shape[0]
    total_rows = e_cols.shape[0]
    devices = lax.axis_size("row")
    smem = pl.BlockSpec(memory_space=pltpu.SMEM)
    hbm = pl.BlockSpec(memory_space=pl.ANY)

    def blocks(count, kind=BF16):
        return pltpu.VMEM((count, blk, blk), kind)

    shape = jax.ShapeDtypeStruct((own, blk, blk), F32)
    deviation, half_response = pl.pallas_call(
        functools.partial(kernel, total_rows, devices),
        out_shape=(shape, shape),
        in_specs=[smem] * 4 + [hbm] * 4,
        out_specs=(hbm, hbm),
        scratch_shapes=[
            blocks(5 * own + 1),
            blocks(3 * own + 1),
            blocks(3 * own + 1),
            blocks(3 * own + 1),
            blocks(3 * own + 1),
            blocks(3 * own + 1),
            blocks(own),
            blocks(own, F32),
            blocks(3 * own, F32),
            blocks(own),
            blocks(owned),
            blocks(owned + 9),
            pltpu.VMEM((2, 4, blk, blk), BF16),
            pltpu.VMEM((2,) + dh_source.shape, jnp.int32),
            pltpu.SMEM((2,) + dh_source.shape, jnp.int32),
            pltpu.SMEM((24 * slots * slots,), jnp.int32),
            blocks(own, F32),
            blocks(own, F32),
            pltpu.SemaphoreType.DMA((8,)),
            pltpu.SemaphoreType.DMA((14,)),
            pltpu.SemaphoreType.DMA((14,)),
        ],
        compiler_params=pltpu.CompilerParams(
            collective_id=0, has_side_effects=True, vmem_limit_bytes=VMEM_BYTES
        ),
        cost_estimate=pl.CostEstimate(
            flops=16 * 2 * own * slots * blk**3, bytes_accessed=4 * 2**20, transcendentals=0
        ),
        name="purify",
    )(
        e_cols,
        p1_cols,
        dh_source,
        dh_slot,
        dh_source,
        e_blocks.reshape(own, blk, blk),
        p1_blocks.reshape(own, blk, blk),
        dh_owned,
    )
    e_out = deviation * math.sqrt(KB * BLK)
    p1_out = half_response * 2.0
    return (e_out.reshape(e_blocks.shape), p1_out.reshape(p1_blocks.shape))


def solution(mesh):
    in_specs = (
        P(("cell", "row"), None, None, None),
        P("cell", None),
        P(("cell", "row"), None, None, None),
        P("cell", None),
        P(("cell", "row"), None, None),
        P(("cell", "row"), None),
        P(("cell", "row"), None),
    )
    out_specs = (P(("cell", "row"), None, None, None), P(("cell", "row"), None, None, None))
    return jax.shard_map(body, mesh=mesh, in_specs=in_specs, out_specs=out_specs, check_vma=False)
```

time: 120 us -> 76.8 us (0.64)
  the two profiles are of different devices: /device:TPU:0 before, /device:TPU:1 now
where the time goes in v1:
time: 76.8 us; the launch traced here: 76.5 us
  Pallas kernels  69.2 us (90%)
  local copies, waits for them, and re-layouts  5.13 us (7%)
  other arithmetic  1.49 us (2%)
    pallas_call x1, Pallas kernels, body(): pl.pallas_call(functools.partial(kernel, total_rows, devices), out_shape=...  69.2 us
    unnamed x16, local copies, waits for them, and re-layouts  5.13 us

profile of v1, /device:TPU:1, one launch (start us, length us, event | category | flops | bytes accessed | tf_op | source)
XLA Modules:
  0.0 76.5 jit_solution(16666027853088085145)
XLA Ops:
  0.6 0.0 copy-start.5
  0.6 0.7 copy-done.5
  1.3 0.0 copy-start.6
  1.3 0.1 copy.9.e_cols
  1.4 0.6 copy-done.6
  2.0 0.0 copy-start.3
  2.0 0.0 copy-start.4
  2.0 0.1 copy.10.p1_cols
  2.1 0.6 copy-done.3
  2.7 0.0 copy-done.4
  2.7 0.0 copy-start
  2.7 1.0 %copy-done = bf16[4,4,128,128]{3,2,1,0:T(8,128)(2,1)S(1)} copy-done((bf16[4,4,128,128]{3,2,1,0:T(8,128)(2,1)S(1)}, bf16[4,4,128,128]{3,2,1,0:T(8,128)(2,1)}, u32[]{:S(2)}) %copy-start) | copy-done | bytes 524312
  3.7 0.0 copy-start.1
  3.7 1.0 %copy-done.1 = bf16[4,4,128,128]{3,2,1,0:T(8,128)(2,1)S(1)} copy-done((bf16[4,4,128,128]{3,2,1,0:T(8,128)(2,1)S(1)}, bf16[4,4,128,128]{3,2,1,0:T(8,128)(2,1)}, u32[]{:S(2)}) %copy-start.1) | copy-done | bytes 524312
  4.8 0.0 copy-start.2
  4.8 1.0 %copy-done.2 = bf16[12,128,128]{2,1,0:T(8,128)(2,1)S(1)} copy-done((bf16[12,128,128]{2,1,0:T(8,128)(2,1)S(1)}, bf16[12,128,128]{2,1,0:T(8,128)(2,1)}, u32[]{:S(2)}) %copy-start.2) | copy-done | bytes 393240
  5.8 69.2 %purify.1 = (f32[16,128,128]{2,1,0:T(8,128)S(1)}, f32[16,128,128]{2,1,0:T(8,128)S(1)}) custom-call(s32[64,4]{1,0:T(8,128)S(1)} %copy.9.e_cols, s32[64,4]{1,0:T(8,128)S(1)} %copy.10.p1_cols, s32[4,3]{1,0:T(4,128)S(1)} %copy-done.3, s32[4,3]{1,0:T(4,128)S(1)} %copy-done.4, s32[4,3]{1,0:T(4,128)S(1)} %copy-done.3, bf16[16,128,128]{2,1,0:T(8,128)(2,1)S(1)} %bitcast.4, ...), custom_call_target="tpu_custom_call" | custom-call | flops 4294967296 | bytes 4194304 | tf_op jit(solution)/shard_map/purify/pallas_call | solution.py:347
  75.0 1.5 %broadcast_multiply_fusion = (f32[16,128,128]{2,1,0:T(8,128)}, f32[16,128,128]{2,1,0:T(8,128)}) fusion(f32[16,128,128]{2,1,0:T(8,128)S(1)} %get-tuple-element.5, f32[16,128,128]{2,1,0:T(8,128)S(1)} %get-tuple-element.4), kind=kLoop, calls=%fused_computation | loop fusion | flops 524288 | bytes 4194304 | tf_op jit(solution)/shard_map/mul | solution.py:393
Async XLA Ops:
  0.6 0.7 copy-start.5
  1.3 0.7 copy-start.6
  2.0 0.7 copy-start.3
  2.0 0.7 copy-start.4
  2.7 1.0 %copy-start = (bf16[4,4,128,128]{3,2,1,0:T(8,128)(2,1)S(1)}, bf16[4,4,128,128]{3,2,1,0:T(8,128)(2,1)}, u32[]{:S(2)}) copy-start(bf16[4,4,128,128]{3,2,1,0:T(8,128)(2,1)} %param.7) | copy-start | bytes 1572868
  3.7 1.0 %copy-start.1 = (bf16[4,4,128,128]{3,2,1,0:T(8,128)(2,1)S(1)}, bf16[4,4,128,128]{3,2,1,0:T(8,128)(2,1)}, u32[]{:S(2)}) copy-start(bf16[4,4,128,128]{3,2,1,0:T(8,128)(2,1)} %param.9) | copy-start | bytes 1572868
  4.8 1.0 %copy-start.2 = (bf16[12,128,128]{2,1,0:T(8,128)(2,1)S(1)}, bf16[12,128,128]{2,1,0:T(8,128)(2,1)}, u32[]{:S(2)}) copy-start(bf16[12,128,128]{2,1,0:T(8,128)(2,1)} %dh_hbm.1) | copy-start | bytes 1179652

commit v2 on v1

v2 whole, which is shorter than its diff:
```python
import functools
import math

import jax
import jax.numpy as jnp
from jax import lax
from jax.experimental import pallas as pl
from jax.experimental.pallas import tpu as pltpu
from jax.sharding import PartitionSpec as P

BLK = 128
REACH = 4
KB = 4
KD = 3
F32 = jnp.float32
BF16 = jnp.bfloat16
MESH = pl.DeviceIdType.MESH
CHUNKS = 2
N_REMOTE = 7 + 8 * CHUNKS
VMEM_BYTES = 56 * 1024 * 1024


def kernel(
    total_rows,
    devices,
    e_cols,
    p1_cols,
    dh_source,
    dh_slot,
    source_hbm,
    e_hbm,
    p1_hbm,
    dh_hbm,
    e_out,
    p1_out,
    dev_wide,
    resp_wide,
    square_wide,
    next_wide,
    next_square,
    next_resp,
    left_prod,
    resp_f32,
    next_f32,
    p1_own,
    dh_own,
    dh_near,
    stage,
    source_vmem,
    source_smem,
    table,
    e_stage,
    p1_stage,
    local_sem,
    send_sem,
    recv_sem,
):
    rows = REACH
    own = rows * KB
    owned = rows * KD
    wide = 7 * own
    centre = 3 * own
    me = lax.axis_index("row")
    core = lax.rem(me, 2)
    odd = lax.rem(lax.div(me, 2), 2)

    def device(step):
        return lax.rem(me + step + devices, devices)

    above, below = device(1), device(-1)
    cross, to_mate = 2 - 4 * odd, 1 - 2 * core
    mate, pair, onward = device(to_mate), device(cross), device(2 * cross)
    backward, diag, far = device(-2 * cross), device(-to_mate), device(6 * core - 3)

    def local(src, dst, sem):
        return pltpu.make_async_copy(src, dst, local_sem.at[sem])

    sems = iter(range(N_REMOTE))

    def remote(src, dst, target):
        sem = next(sems)
        return pltpu.make_async_remote_copy(
            src_ref=src,
            dst_ref=dst,
            send_sem=send_sem.at[sem],
            recv_sem=recv_sem.at[sem],
            device_id={"row": target},
            device_id_type=MESH,
        )

    def at_slot(ref, step, chunk=0, chunks=1):
        size = own // chunks
        return ref.at[pl.ds(centre + step * own + chunk * size, size)]

    get_e = local(e_hbm, at_slot(dev_wide, 0), 0)
    get_p1 = local(p1_hbm, p1_own, 1)
    get_dh = local(dh_hbm, dh_own, 2)
    get_near = local(dh_hbm, dh_near.at[pl.ds(4, owned)], 3)
    get_e.start()
    get_dh.start()
    get_p1.start()
    get_near.start()

    barrier = pltpu.get_barrier_semaphore()
    for neighbour in (mate, pair, onward, backward, diag, far):
        pl.semaphore_signal(
            barrier, inc=1, device_id={"row": neighbour}, device_id_type=MESH
        )
    pl.semaphore_wait(barrier, 6)

    src_up = remote(source_hbm, source_vmem.at[0], above)
    src_down = remote(source_hbm, source_vmem.at[1], below)
    src_up.start()
    src_down.start()

    class Spread:
        def __init__(self, ref, src, reach_far):
            self.ref, self.waits = ref, []
            size = own // CHUNKS
            self.crossing = [
                remote(
                    src(c * size, size), at_slot(ref, -cross, c, CHUNKS), pair
                )
                for c in range(CHUNKS)
            ]
            self.others = [remote(src(0, own), at_slot(ref, -to_mate), mate)]
            if reach_far:
                self.others.append(
                    remote(src(0, own), at_slot(ref, 3 - 6 * core), far)
                )
            for copy in self.crossing + self.others:
                copy.start()
            self.passed = []

        def pass_on(self, c):
            ref = self.ref
            self.crossing[c].wait_recv()
            held = at_slot(ref, cross, c, CHUNKS)
            passed = remote(held, at_slot(ref, -cross, c, CHUNKS), onward)
            shared = remote(held, at_slot(ref, cross - to_mate, c, CHUNKS), mate)
            passed.start()
            shared.start()
            self.passed.append(passed)
            self.others.append(shared)

        def share(self, c):
            ref = self.ref
            self.passed[c].wait_recv()
            shared = remote(
                at_slot(ref, -cross, c, CHUNKS),
                at_slot(ref, -cross - to_mate, c, CHUNKS),
                mate,
            )
            shared.start()
            self.others.append(shared)

        def finish(self):
            for copy in self.crossing + self.passed:
                copy.wait_send()
            for copy in self.others:
                copy.wait()

    dev = Spread(dev_wide, lambda first, size: e_hbm.at[pl.ds(first, size)], True)

    zero = jnp.zeros((BLK, BLK), BF16)
    for ref in (dev_wide, resp_wide, square_wide, next_wide, next_square, next_resp):
        ref[wide] = zero
    dh_near[owned + 8] = zero

    src_up.wait()
    src_down.wait()
    for side in range(2):
        to_smem = local(source_vmem.at[side], source_smem.at[side], 4 + side)
        to_smem.start()
        to_smem.wait()
    get_dh.wait()

    def fill_stage(side):
        count = jnp.int32(0)
        picked = [jnp.int32(0)] * 4
        for row in range(rows):
            for u in range(KD):
                position = source_smem[side, row, u]
                mine = lax.div(position, owned) == me
                here = position - me * owned
                for slot in range(4):
                    hit = jnp.logical_and(mine, count == slot)
                    picked[slot] = jnp.where(hit, here, picked[slot])
                count = count + jnp.where(mine, 1, 0)
        for slot in range(4):
            stage[side, slot] = dh_own[picked[slot]]

    fill_stage(0)
    fill_stage(1)
    dh_down = remote(stage.at[0], dh_near.at[pl.ds(owned + 4, 4)], below)
    dh_up = remote(stage.at[1], dh_near.at[pl.ds(0, 4)], above)
    dh_down.start()
    dh_up.start()

    def fill(base, left, right, target):
        def one(i, carry):
            row = lax.rem(row_start - 3 * REACH + i + total_rows, total_rows)
            wanted = [target[row, n] for n in range(KB)]
            for k in range(KB):
                col = left[row, k]
                near = lax.rem(col - row_start + 3 * REACH + total_rows, total_rows)
                held = [right[col, m] for m in range(KB)]
                for n in range(KB):
                    at = jnp.int32(wide)
                    for m in range(KB):
                        at = jnp.where(held[m] == wanted[n], near * KB + m, at)
                    table[base + i * KB * KB + k * KB + n] = jnp.clip(at, 0, wide)
            return carry

        return one

    row_start = me * rows
    ee, ep, pe = (kind * wide * KB for kind in range(3))
    lax.fori_loop(4, 24, fill(ee, e_cols, e_cols, e_cols), 0)
    for c in range(CHUNKS):
        dev.pass_on(c)

    get_p1.wait()
    get_near.wait()
    dh_down.wait()
    dh_up.wait()
    from_below, from_above = jnp.int32(0), jnp.int32(0)
    for row in range(rows):
        at = [jnp.int32(owned + 8)] * KB
        for u in range(KD):
            position = dh_source[row, u]
            owner = lax.div(position, owned)
            is_below, is_above = owner == below, owner == above
            place = jnp.where(
                is_below,
                from_below,
                jnp.where(is_above, owned + 4 + from_above, 4 + position - me * owned),
            )
            place = jnp.clip(place, 0, owned + 8)
            from_below = from_below + jnp.where(is_below, 1, 0)
            from_above = from_above + jnp.where(is_above, 1, 0)
            slot = dh_slot[row, u]
            for m in range(KB):
                at[m] = jnp.where(slot == m, place, at[m])
        for m in range(KB):
            q = row * KB + m
            value = p1_own[q].astype(F32) + dh_near[at[m]].astype(F32)
            resp_f32[q] = value
            resp_wide[centre + q] = value.astype(BF16)
    resp = Spread(
        resp_wide, lambda first, size: resp_wide.at[pl.ds(centre + first, size)], False
    )
    lax.fori_loop(8, 20, fill(ep, e_cols, p1_cols, p1_cols), 0)
    lax.fori_loop(8, 20, fill(pe, p1_cols, e_cols, p1_cols), 0)
    for c in range(CHUNKS):
        dev.share(c)

    def product(i, terms, sink):
        for pair_n in range(KB // 2):
            acc = None
            for left, right, base in terms:
                for half in range(KB // 2):
                    ks = (2 * half, 2 * half + 1)
                    ns = (2 * pair_n, 2 * pair_n + 1)
                    a = jnp.concatenate([left[i * KB + k] for k in ks], axis=1)
                    b = jnp.concatenate(
                        [
                            jnp.concatenate(
                                [right[table[base + i * KB * KB + k * KB + n]] for n in ns],
                                axis=1,
                            )
                            for k in ks
                        ],
                        axis=0,
                    )
                    part = jnp.dot(a, b, preferred_element_type=F32)
                    acc = part if acc is None else acc + part
            for j in range(2):
                sink(i * KB + 2 * pair_n + j, acc[:, j * BLK : (j + 1) * BLK])

    def run(first, last, terms, sink):
        def one(i, carry):
            product(i, terms, sink)
            return carry

        lax.fori_loop(first, last, one, 0)

    get_e.wait()
    dev.finish()

    def into(ref):
        def sink(q, value):
            ref[q] = value.astype(BF16)

        return sink

    run(4, 24, [(dev_wide, dev_wide, ee)], into(square_wide))

    def to_next(q, value):
        next_wide[q] = (1.5 * dev_wide[q].astype(F32) - 2.0 * value).astype(BF16)

    def to_next_own(q, value):
        new = 1.5 * dev_wide[q].astype(F32) - 2.0 * value
        next_f32[q - centre] = new
        next_wide[q] = new.astype(BF16)

    cube = [(square_wide, dev_wide, ee)]
    resp.pass_on(0)
    run(4, 12, cube, to_next)
    for c in range(1, CHUNKS):
        resp.pass_on(c)
    run(12, 16, cube, to_next_own)
    run(16, 24, cube, to_next)
    run(8, 20, [(next_wide, next_wide, ee)], into(next_square))

    def to_e(q, value):
        e_stage[q - centre] = 1.5 * next_f32[q - centre] - 2.0 * value

    run(12, 16, [(next_square, next_wide, ee)], to_e)
    put_e = local(e_stage, e_out, 6)
    put_e.start()
    for c in range(CHUNKS):
        resp.share(c)
    resp.finish()

    run(8, 20, [(dev_wide, resp_wide, ep)], into(left_prod))

    def to_resp(q, value):
        next_resp[q] = (1.5 * resp_wide[q].astype(F32) - 2.0 * value).astype(BF16)

    def to_resp_own(q, value):
        new = 1.5 * resp_f32[q - centre] - 2.0 * value
        resp_f32[q - centre] = new
        next_resp[q] = new.astype(BF16)

    terms = [
        (square_wide, resp_wide, ep),
        (left_prod, dev_wide, pe),
        (resp_wide, square_wide, pe),
    ]
    run(8, 12, terms, to_resp)
    run(12, 16, terms, to_resp_own)
    run(16, 20, terms, to_resp)

    run(12, 16, [(next_wide, next_resp, ep)], into(left_prod))

    def to_out(q, value):
        p1_stage[q - centre] = 0.75 * resp_f32[q - centre] - value

    run(
        12,
        16,
        [
            (next_square, next_resp, ep),
            (left_prod, next_wide, pe),
            (next_resp, next_square, pe),
        ],
        to_out,
    )
    put_p1 = local(p1_stage, p1_out, 7)
    put_p1.start()
    put_e.wait()
    put_p1.wait()


def body(e_blocks, e_cols, p1_blocks, p1_cols, dh_owned, dh_source, dh_slot):
    rows, slots, blk = e_blocks.shape[:3]
    own = rows * slots
    owned = dh_owned.shape[0]
    total_rows = e_cols.shape[0]
    devices = lax.axis_size("row")
    smem = pl.BlockSpec(memory_space=pltpu.SMEM)
    hbm = pl.BlockSpec(memory_space=pltpu.HBM)

    def blocks(count, kind=BF16):
        return pltpu.VMEM((count, blk, blk), kind)

    shape = jax.ShapeDtypeStruct((own, blk, blk), F32)
    deviation, half_response = pl.pallas_call(
        functools.partial(kernel, total_rows, devices),
        out_shape=(shape, shape),
        in_specs=[smem] * 4 + [hbm] * 4,
        out_specs=(hbm, hbm),
        scratch_shapes=[
            *[blocks(7 * own + 1)] * 6,
            blocks(7 * own),
            blocks(own, F32),
            blocks(own, F32),
            blocks(own),
            blocks(owned),
            blocks(owned + 9),
            pltpu.VMEM((2, 4, blk, blk), BF16),
            pltpu.VMEM((2,) + dh_source.shape, jnp.int32),
            pltpu.SMEM((2,) + dh_source.shape, jnp.int32),
            pltpu.SMEM((3 * 7 * own * slots,), jnp.int32),
            blocks(own, F32),
            blocks(own, F32),
            pltpu.SemaphoreType.DMA((8,)),
            pltpu.SemaphoreType.DMA((N_REMOTE,)),
            pltpu.SemaphoreType.DMA((N_REMOTE,)),
        ],
        compiler_params=pltpu.CompilerParams(
            collective_id=0, has_side_effects=True, vmem_limit_bytes=VMEM_BYTES
        ),
        cost_estimate=pl.CostEstimate(
            flops=30 * 2 * own * slots * blk**3, bytes_accessed=4 * 2**20, transcendentals=0
        ),
        name="purify",
    )(
        e_cols,
        p1_cols,
        dh_source,
        dh_slot,
        dh_source,
        e_blocks.reshape(own, blk, blk),
        p1_blocks.reshape(own, blk, blk),
        dh_owned,
    )
    e_out = deviation * math.sqrt(KB * BLK)
    p1_out = half_response * 2.0
    return (e_out.reshape(e_blocks.shape), p1_out.reshape(p1_blocks.shape))


def solution(mesh):
    in_specs = (
        P(("cell", "row"), None, None, None),
        P("cell", None),
        P(("cell", "row"), None, None, None),
        P("cell", None),
        P(("cell", "row"), None, None),
        P(("cell", "row"), None),
        P(("cell", "row"), None),
    )
    out_specs = (P(("cell", "row"), None, None, None), P(("cell", "row"), None, None, None))
    return jax.shard_map(body, mesh=mesh, in_specs=in_specs, out_specs=out_specs, check_vma=False)
```

time: 76.8 us -> 71.2 us (0.927)
  the two profiles are of different devices: /device:TPU:1 before, /device:TPU:0 now
where the time goes in v2:
time: 71.2 us; the launch traced here: 70.8 us
  Pallas kernels  65 us (91%)
  other arithmetic  3.13 us (4%)
  local copies, waits for them, and re-layouts  2.1 us (3%)
    pallas_call x1, Pallas kernels, body(): pl.pallas_call(functools.partial(kernel, total_rows, devices), out_shape=...  65 us
    mul x1, other arithmetic, body(): p1_out = half_response * 2.0  3.13 us
    unnamed x6, local copies, waits for them, and re-layouts  2.1 us

profile of v2, /device:TPU:0, one launch (start us, length us, event | category | flops | bytes accessed | tf_op | source)
XLA Modules:
  0.0 70.8 jit_solution(16409309849887871104)
XLA Ops:
  0.6 0.0 copy-start
  0.6 0.7 copy-done
  1.3 0.0 copy-start.1
  1.3 0.7 %copy.9.e_cols = s32[64,4]{1,0:T(8,128)} copy(s32[64,4]{0,1:T(4,128)S(1)} %copy-done) | data formatting | bytes 2048 | tf_op args[1]
  2.0 0.0 copy-done.1
  2.0 0.7 %copy.10.p1_cols = s32[64,4]{1,0:T(8,128)} copy(s32[64,4]{0,1:T(4,128)S(1)} %copy-done.1) | data formatting | bytes 2048 | tf_op args[3]
  2.7 65.0 %purify.1 = (f32[16,128,128]{2,1,0:T(8,128)}, f32[16,128,128]{2,1,0:T(8,128)}) custom-call(s32[64,4]{1,0:T(8,128)} %copy.9.e_cols, s32[64,4]{1,0:T(8,128)} %copy.10.p1_cols, s32[4,3]{1,0:T(4,128)} %source_hbm.1, s32[4,3]{1,0:T(4,128)} %dh_slot.1, s32[4,3]{1,0:T(4,128)} %source_hbm.1, bf16[16,128,128]{2,1,0:T(8,128)(2,1)} %bitcast.6, ...), custom_call_target="tpu_custom_call" | custom-call | flops 8053063680 | bytes 4194304 | tf_op jit(solution)/shard_map/purify/pallas_call | solution.py:379
  67.7 3.1 %broadcast_multiply_fusion = (f32[16,128,128]{2,1,0:T(8,128)}, f32[16,128,128]{2,1,0:T(8,128)}) fusion(f32[16,128,128]{2,1,0:T(8,128)} %get-tuple-element.5, f32[16,128,128]{2,1,0:T(8,128)} %get-tuple-element.4), kind=kLoop, calls=%fused_computation | loop fusion | flops 524288 | bytes 4194304 | tf_op jit(solution)/shard_map/mul | solution.py:420
Async XLA Ops:
  0.6 0.7 copy-start
  1.3 0.7 %copy-start.1 = (s32[64,4]{0,1:T(4,128)S(1)}, s32[64,4]{0,1:T(4,128)}, u32[]{:S(2)}) copy-start(s32[64,4]{0,1:T(4,128)} %param.10) | copy-start | bytes 3076

commit v3 on v2

--- a/solution.py
+++ b/solution.py
@@ -16,6 +16,7 @@
 BF16 = jnp.bfloat16
 MESH = pl.DeviceIdType.MESH
 CHUNKS = 2
+UNROLL = 4
 N_REMOTE = 7 + 8 * CHUNKS
 VMEM_BYTES = 56 * 1024 * 1024
 
@@ -181,8 +182,8 @@
         for row in range(rows):
             for u in range(KD):
                 position = source_smem[side, row, u]
-                mine = lax.div(position, owned) == me
                 here = position - me * owned
+                mine = jnp.logical_and(here >= 0, here < owned)
                 for slot in range(4):
                     hit = jnp.logical_and(mine, count == slot)
                     picked[slot] = jnp.where(hit, here, picked[slot])
@@ -197,18 +198,22 @@
     dh_down.start()
     dh_up.start()
 
+    def around(row):
+        row = jnp.where(row < 0, row + total_rows, row)
+        return jnp.where(row >= total_rows, row - total_rows, row)
+
     def fill(base, left, right, target):
         def one(i, carry):
-            row = lax.rem(row_start - 3 * REACH + i + total_rows, total_rows)
+            row = around(row_start - 3 * REACH + i)
             wanted = [target[row, n] for n in range(KB)]
             for k in range(KB):
                 col = left[row, k]
-                near = lax.rem(col - row_start + 3 * REACH + total_rows, total_rows)
+                start = around(col - row_start + 3 * REACH) * KB
                 held = [right[col, m] for m in range(KB)]
                 for n in range(KB):
                     at = jnp.int32(wide)
                     for m in range(KB):
-                        at = jnp.where(held[m] == wanted[n], near * KB + m, at)
+                        at = jnp.where(held[m] == wanted[n], start + m, at)
                     table[base + i * KB * KB + k * KB + n] = jnp.clip(at, 0, wide)
             return carry
 
@@ -216,7 +221,6 @@
 
     row_start = me * rows
     ee, ep, pe = (kind * wide * KB for kind in range(3))
-    lax.fori_loop(4, 24, fill(ee, e_cols, e_cols, e_cols), 0)
     for c in range(CHUNKS):
         dev.pass_on(c)
 
@@ -229,8 +233,9 @@
         at = [jnp.int32(owned + 8)] * KB
         for u in range(KD):
             position = dh_source[row, u]
-            owner = lax.div(position, owned)
-            is_below, is_above = owner == below, owner == above
+            in_below, in_above = position - below * owned, position - above * owned
+            is_below = jnp.logical_and(in_below >= 0, in_below < owned)
+            is_above = jnp.logical_and(in_above >= 0, in_above < owned)
             place = jnp.where(
                 is_below,
                 from_below,
@@ -250,6 +255,7 @@
     resp = Spread(
         resp_wide, lambda first, size: resp_wide.at[pl.ds(centre + first, size)], False
     )
+    lax.fori_loop(4, 24, fill(ee, e_cols, e_cols, e_cols), 0)
     lax.fori_loop(8, 20, fill(ep, e_cols, p1_cols, p1_cols), 0)
     lax.fori_loop(8, 20, fill(pe, p1_cols, e_cols, p1_cols), 0)
     for c in range(CHUNKS):
@@ -283,9 +289,11 @@
             product(i, terms, sink)
             return carry
 
-        lax.fori_loop(first, last, one, 0)
+        lax.fori_loop(first, last, one, 0, unroll=UNROLL)
 
     get_e.wait()
+    for c in range(CHUNKS):
+        resp.pass_on(c)
     dev.finish()
 
     def into(ref):
@@ -305,10 +313,7 @@
         next_wide[q] = new.astype(BF16)
 
     cube = [(square_wide, dev_wide, ee)]
-    resp.pass_on(0)
     run(4, 12, cube, to_next)
-    for c in range(1, CHUNKS):
-        resp.pass_on(c)
     run(12, 16, cube, to_next_own)
     run(16, 24, cube, to_next)
     run(8, 20, [(next_wide, next_wide, ee)], into(next_square))

time: 71.2 us -> 60.9 us (0.86)
  Pallas kernels: 65 us -> 54.7 us
    pallas_call x1, Pallas kernels: 65 us -> 54.7 us  [body(): pl.pallas_call(functools.partial(kernel, total_rows, devices), out_shape=...]
where the time goes in v3:
time: 60.9 us; the launch traced here: 60.6 us
  Pallas kernels  54.7 us (90%)
  other arithmetic  3.13 us (5%)
  local copies, waits for them, and re-layouts  2.1 us (3%)
  between operations  0.65 us (1%)
    pallas_call x1, Pallas kernels, body(): pl.pallas_call(functools.partial(kernel, total_rows, devices), out_shape=...  54.7 us
    mul x1, other arithmetic, body(): p1_out = half_response * 2.0  3.13 us
    unnamed x6, local copies, waits for them, and re-layouts  2.1 us

profile of v3, /device:TPU:0, one launch (start us, length us, event | category | flops | bytes accessed | tf_op | source)
XLA Modules:
  0.0 60.6 jit_solution(11570279220359485036)
XLA Ops:
  0.6 0.0 copy-start
  0.6 0.7 %copy-done = s32[64,4]{0,1:T(4,128)S(1)} copy-done((s32[64,4]{0,1:T(4,128)S(1)}, s32[64,4]{0,1:T(4,128)}, u32[]{:S(2)}) %copy-start) | copy-done | bytes 1048
  1.3 0.0 copy-start.1
  1.3 0.7 %copy.9.e_cols = s32[64,4]{1,0:T(8,128)} copy(s32[64,4]{0,1:T(4,128)S(1)} %copy-done) | data formatting | bytes 2048 | tf_op args[1]
  2.0 0.0 copy-done.1
  2.0 0.7 %copy.10.p1_cols = s32[64,4]{1,0:T(8,128)} copy(s32[64,4]{0,1:T(4,128)S(1)} %copy-done.1) | data formatting | bytes 2048 | tf_op args[3]
  2.7 54.7 %purify.1 = (f32[16,128,128]{2,1,0:T(8,128)}, f32[16,128,128]{2,1,0:T(8,128)}) custom-call(s32[64,4]{1,0:T(8,128)} %copy.9.e_cols, s32[64,4]{1,0:T(8,128)} %copy.10.p1_cols, s32[4,3]{1,0:T(4,128)} %source_hbm.1, s32[4,3]{1,0:T(4,128)} %dh_slot.1, s32[4,3]{1,0:T(4,128)} %source_hbm.1, bf16[16,128,128]{2,1,0:T(8,128)(2,1)} %bitcast.6, ...), custom_call_target="tpu_custom_call" | custom-call | flops 8053063680 | bytes 4194304 | tf_op jit(solution)/shard_map/purify/pallas_call | solution.py:384
  57.5 3.1 %broadcast_multiply_fusion = (f32[16,128,128]{2,1,0:T(8,128)}, f32[16,128,128]{2,1,0:T(8,128)}) fusion(f32[16,128,128]{2,1,0:T(8,128)} %get-tuple-element.5, f32[16,128,128]{2,1,0:T(8,128)} %get-tuple-element.4), kind=kLoop, calls=%fused_computation | loop fusion | flops 524288 | bytes 4194304 | tf_op jit(solution)/shard_map/mul | solution.py:425
Async XLA Ops:
  0.6 0.7 %copy-start = (s32[64,4]{0,1:T(4,128)S(1)}, s32[64,4]{0,1:T(4,128)}, u32[]{:S(2)}) copy-start(s32[64,4]{0,1:T(4,128)} %param.8) | copy-start | bytes 3076
  1.3 0.7 %copy-start.1 = (s32[64,4]{0,1:T(4,128)S(1)}, s32[64,4]{0,1:T(4,128)}, u32[]{:S(2)}) copy-start(s32[64,4]{0,1:T(4,128)} %param.10) | copy-start | bytes 3076
